TPU v7x, 256 devices: a whole 4x4x8 slice. The times are simulated.
256 devices in a mesh: pencil: 16 (over x, y), band: 16 (over z, core).
Axes of the slice: x: 4, y: 4, z: 8, core: 2. Of those that a mesh axis runs over, the one named last changes fastest.
Arguments:
- coeffs: float32 [16, 512, 224], P('band', 'pencil'), may hold values from -16 to 16
- columns: int32 [512], replicated, may hold values from 0 to 12543, as said below
- potential: float32 [112, 12544], P('pencil'), may hold values from -5 to 5
- ritz_vectors: float32 [2, 16, 16], replicated, may hold values from -1 to 2
Outputs:
- refined_coeffs: float32 [16, 512, 224], P('band', 'pencil')
- refined_hcoeffs: float32 [16, 512, 224], P('band', 'pencil')
- ritz_values: float32 [16], replicated
Inputs may be any that keep to these rules, and one draw needn't show every extreme that they name: The 512 entries are distinct columns ix * 112 + iy with f(ix)^2 + f(iy)^2 <= 28^2; stick s belongs to pencil device s // 32.
All inputs are finite; a program needn't handle non-finite values.
Results may differ from a plain program's by a relative error of at most 0.0003.
Values sent between devices are 32-bit elements; how exact they have to be, the bound alone decides.
A program may use at most 64 MiB of HBM per device.

v0:
```python
import functools

import jax
import jax.numpy as jnp
from jax import lax
from jax.sharding import Mesh
from jax.sharding import PartitionSpec as P

PENCIL = ("pencil_0", "pencil_1")
BAND = ("band_0", "band_1")
PENCIL_BAND = ("pencil_0", "pencil_1", "band_0", "band_1")


precise = lax.Precision.HIGHEST


def sent_together(arrays, axis, split_dim, concat_dim, along):
    ends, at = ([], 0)
    for a in arrays[:-1]:
        at += a.shape[along]
        ends.append(at)
    both = jnp.concatenate(arrays, axis=along)
    return tuple(
        jnp.split(
            lax.all_to_all(both, axis, split_axis=split_dim, concat_axis=concat_dim, tiled=True),
            ends,
            axis=along,
        )
    )


def one_axis_at_a_time(x, axes):
    return functools.reduce(lax.psum, axes, x)


def frequencies(indices, length):
    return jnp.where(indices < length // 2, indices, indices - length)


def kinetic_table(columns, grid_size):
    radius = grid_size // 4
    wave_x = frequencies(columns // grid_size, grid_size).astype(jnp.float32)
    wave_y = frequencies(columns % grid_size, grid_size).astype(jnp.float32)
    wave_z = frequencies(jnp.arange(grid_size, dtype=jnp.int32), grid_size).astype(jnp.float32)
    lateral = wave_x * wave_x + wave_y * wave_y
    return 0.5 * (lateral[:, None] + (wave_z * wave_z)[None, :]) / float(radius * radius)


def dft_tables(length, direction):
    indices = jnp.arange(length, dtype=jnp.int32)
    phases = indices[:, None] * indices[None, :] % length
    angles = 2.0 * jnp.pi / length * phases.astype(jnp.float32)
    cosine = jnp.cos(angles)
    sine_table = direction * jnp.sin(angles)
    upper_rows = jnp.stack([cosine, sine_table], axis=1)
    lower_rows = jnp.stack([-sine_table, cosine], axis=1)
    return jnp.stack([upper_rows, lower_rows], axis=0)


def flatten(values):
    band_total = values.shape[0]
    half_width = values.shape[-1] // 2
    turned = jnp.concatenate([values[..., half_width:], -values[..., :half_width]], axis=-1)
    return (values.reshape(band_total, -1), turned.reshape(band_total, -1))


def partial_gram(flat_values, members):
    stacked = jnp.concatenate(members, axis=0)
    return lax.dot_general(flat_values, stacked, (((1,), (1,)), ((), ())), precision=precise)


def complex_product(left_real, left_imag, right_real, right_imag):
    out_real = jnp.dot(left_real, right_real, precision=precise) - jnp.dot(
        left_imag, right_imag, precision=precise
    )
    out_imag = jnp.dot(left_real, right_imag, precision=precise) + jnp.dot(
        left_imag, right_real, precision=precise
    )
    return (out_real, out_imag)


def refine(over_real, over_imag, ham_real, ham_imag, vector_real, vector_imag):
    band_total = vector_real.shape[0]
    adjoint_real = vector_real.T
    adjoint_imag = -vector_imag.T
    temp_real, temp_imag = complex_product(over_real, over_imag, vector_real, vector_imag)
    metric_real, metric_imag = complex_product(adjoint_real, adjoint_imag, temp_real, temp_imag)
    temp_real, temp_imag = complex_product(ham_real, ham_imag, vector_real, vector_imag)
    energy_real, energy_imag = complex_product(adjoint_real, adjoint_imag, temp_real, temp_imag)
    identity = jnp.eye(band_total, dtype=vector_real.dtype)
    residual_real = identity - metric_real
    residual_imag = -metric_imag
    values = jnp.diagonal(energy_real) / jnp.diagonal(metric_real)
    spacing = values[None, :] - values[:, None]
    floor_value = (0.25 / band_total) ** 2
    factor = spacing / jnp.maximum(spacing * spacing, floor_value)
    upper_real = energy_real + values[None, :] * residual_real
    upper_imag = energy_imag + values[None, :] * residual_imag
    on_diagonal = identity > 0.5
    update_real = jnp.where(on_diagonal, 0.5 * residual_real, upper_real * factor)
    update_imag = jnp.where(on_diagonal, 0.5 * residual_imag, upper_imag * factor)
    change_real, change_imag = complex_product(vector_real, vector_imag, update_real, update_imag)
    return (vector_real + change_real, vector_imag + change_imag, values)


def rotate(flat_values, turned_values, new_real, new_imag):
    stacked = jnp.concatenate([flat_values, -turned_values], axis=0)
    weights = jnp.concatenate([new_real, new_imag], axis=0)
    return lax.dot_general(weights, stacked, (((0,), (0,)), ((), ())), precision=precise)


def shards(coeffs, columns, potential, ritz_vectors):
    band_count, stick_count, row_width = coeffs.shape
    grid_size = row_width // 2
    planes_dev = potential.shape[0]
    band_total = ritz_vectors.shape[1]
    potential_planes = potential.reshape(planes_dev, grid_size, grid_size)
    norm_total = float(lax.axis_size(PENCIL) * stick_count * grid_size)
    inverse = dft_tables(grid_size, 1.0)
    forward = dft_tables(grid_size, -1.0)
    stick_start = lax.axis_index(PENCIL) * stick_count
    local_columns = lax.dynamic_slice_in_dim(columns, stick_start, stick_count, 0)
    kinetic = kinetic_table(local_columns, grid_size)
    kinetic_both = jnp.concatenate([kinetic, kinetic], axis=1)
    sticks_four = coeffs.reshape(band_count, stick_count, 2, grid_size)
    zsticks = jnp.einsum("bsck,ckdz->bdzs", sticks_four, inverse, precision=precise)
    received = lax.all_to_all(zsticks, PENCIL, split_axis=2, concat_axis=3, tiled=True)
    row_count = received.shape[0]
    planes = jnp.zeros((row_count, 2, planes_dev, grid_size * grid_size), jnp.float32)
    planes = planes.at[:, :, :, columns].set(received)
    planes = planes.reshape(row_count, 2, planes_dev, grid_size, grid_size)
    planes = jnp.einsum("bczxy,cydv->bdzxv", planes, inverse, precision=precise)
    planes = jnp.einsum("bczxy,cxdu->bdzuy", planes, inverse, precision=precise)
    planes = planes * potential_planes[None, None]
    planes = jnp.einsum("bczxy,cydv->bdzxv", planes, forward, precision=precise)
    planes = jnp.einsum("bczxy,cxdu->bdzuy", planes, forward, precision=precise)
    picked = planes.reshape(row_count, 2, planes_dev, grid_size * grid_size)[:, :, :, columns]
    returned = lax.all_to_all(picked, PENCIL, split_axis=3, concat_axis=2, tiled=True)
    spectrum = jnp.einsum("bcks,ckdz->bsdz", returned, forward, precision=precise)
    spectrum = spectrum.reshape(band_count, stick_count, row_width)
    hcoeffs = spectrum / float(grid_size**3) + kinetic_both[None] * coeffs
    coeffs_t, hcoeffs_t = sent_together((coeffs, hcoeffs), BAND, 1, 0, 2)
    flat_coeffs, turned = flatten(coeffs_t)
    flat_hcoeffs, turned_hcoeffs = flatten(hcoeffs_t)
    grams = one_axis_at_a_time(
        partial_gram(flat_coeffs, (flat_coeffs, turned, flat_hcoeffs, turned_hcoeffs)), PENCIL_BAND
    )
    correlation = grams[:, : 2 * band_total]
    hamiltonian = grams[:, 2 * band_total :]
    correlation = correlation / norm_total
    hamiltonian = hamiltonian / norm_total
    new_real, new_imag, values = refine(
        correlation[:, :band_total],
        correlation[:, band_total:],
        hamiltonian[:, :band_total],
        hamiltonian[:, band_total:],
        ritz_vectors[0],
        ritz_vectors[1],
    )
    rotated = rotate(flat_coeffs, turned, new_real, new_imag).reshape(coeffs_t.shape)
    rotated_h = rotate(flat_hcoeffs, turned_hcoeffs, new_real, new_imag).reshape(hcoeffs_t.shape)
    refined, refined_h = sent_together((rotated, rotated_h), BAND, 0, 1, 2)
    return (refined, refined_h, values)


def solution(mesh):
    torus = Mesh(mesh.devices.reshape(4, 4, 8, 2), ("pencil_0", "pencil_1", "band_0", "band_1"))
    return jax.shard_map(
        shards,
        mesh=torus,
        in_specs=(P(BAND, PENCIL, None), P(), P(PENCIL, None), P()),
        out_specs=(P(BAND, PENCIL, None), P(BAND, PENCIL, None), P()),
        check_vma=False,
    )
```

profile of v0, /device:TPU:1, one launch (start us, length us, event | category | flops | bytes accessed | tf_op | source)
XLA Modules:
  0.0 194.5 jit_solution(10374781039222419597)
XLA Ops:
  0.6 0.3 fusion.49
  0.9 0.2 broadcast_multiply_fusion
  1.1 0.2 fusion.56
  1.4 0.8 reshape.170
  2.3 0.3 convolution_bitcast_fusion.5
  2.7 0.8 reshape.237
  3.4 7.6 %all-to-all-start = ((f32[16,1,448]{2,1,0:T(1,128)}), f32[16,1,448]{2,1,0:T(1,128)S(1)}, u32[]{:S(2)}, u32[]{:S(2)}) async-start(f32[16,1,448]{2,1,0:T(1,128)} %reshape.237), calls=%async_computation | async-start | bytes 65536 | tf_op jit(solution)/shard_map/all_to_all | solution.py:127
  11.1 0.7 compare_select_fusion
  11.8 0.8 fusion.95
  12.5 0.7 fusion.129
  13.4 1.3 mul.218
  14.6 2.9 %all-to-all-done = f32[16,1,448]{2,1,0:T(1,128)S(1)} async-done(((f32[16,1,448]{2,1,0:T(1,128)}), f32[16,1,448]{2,1,0:T(1,128)S(1)}, u32[]{:S(2)}, u32[]{:S(2)}) %all-to-all-start) | async-done | bytes 28704 | tf_op jit(solution)/shard_map/all_to_all | solution.py:127
  17.5 0.5 broadcast.267
  18.0 0.7 reduce.1
  19.0 0.3 copy.88
  19.3 4.9 %broadcast.238 = f32[2,7,12544]{1,0,2:T(2,128)} broadcast(f32[]{:T(128)} %constant.71.clone.1), dimensions={} | broadcast | bytes 702468 | tf_op jit(solution)/shard_map/broadcast_in_dim | solution.py:129
  24.2 47.1 %scatter_fusion = f32[2,7,12544]{1,0,2:T(2,128)} fusion(f32[2,7,12544]{1,0,2:T(2,128)} %broadcast.238, s32[512]{0:T(512)S(1)} %compare_select_fusion, f32[512,2,7]{2,1,0:T(2,128)S(1)} %copy.88), kind=kCustom, calls=%fused_computation.3 | custom fusion | bytes 88064 | tf_op jit(solution)/shard_map/scatter | solution.py:130
  71.3 11.2 %copy.90 = f32[2,7,112,112]{3,2,0,1:T(8,128)S(1)} copy(f32[2,7,112,112]{1,0,3,2:T(2,128)} %bitcast.211) | data formatting | bytes 1404928 | tf_op jit(solution)/shard_map/reshape.3
  82.5 1.6 convolution_bitcast_fusion.3
  84.1 1.6 fusion.1
  85.7 1.6 convolution_bitcast_fusion.2
  87.3 1.6 convolution_bitcast_fusion.1
  88.9 9.4 %copy.138 = f32[1,2,7,112,112]{2,1,4,3,0:T(2,128)} copy(f32[1,2,7,112,112]{4,3,2,1,0:T(8,128)S(1)} %convolution_bitcast_fusion.1) | data formatting | bytes 1404928 | tf_op jit(solution)/shard_map/reshape | solution.py:137
  98.4 6.1 %gather_fusion = f32[512,2,7]{2,1,0:T(2,128)S(1)} fusion(f32[2,7,12544]{1,0,2:T(2,128)} %bitcast.212, s32[1024]{0:T(1024)S(1)} %pad_clamp_fusion), kind=kCustom, calls=%fused_computation | custom fusion | bytes 59392 | tf_op jit(solution)/shard_map/gather | solution.py:137
  104.6 1.5 reshape.239
  106.1 3.8 %all-to-all-start.1 = ((f32[16,1,448]{2,1,0:T(1,128)}), f32[16,1,448]{2,1,0:T(1,128)S(1)}, u32[]{:S(2)}, u32[]{:S(2)}) async-start(f32[16,1,448]{2,1,0:T(1,128)} %reshape.239), calls=%async_computation.1 | async-start | bytes 65536 | tf_op jit(solution)/shard_map/all_to_all | solution.py:138
  110.3 6.0 %all-to-all-done.1 = f32[16,1,448]{2,1,0:T(1,128)S(1)} async-done(((f32[16,1,448]{2,1,0:T(1,128)}), f32[16,1,448]{2,1,0:T(1,128)S(1)}, u32[]{:S(2)}, u32[]{:S(2)}) %all-to-all-start.1) | async-done | bytes 28704 | tf_op jit(solution)/shard_map/all_to_all | solution.py:138
  116.3 0.7 reduce.2
  117.1 0.7 reshape.240
  117.8 0.3 copy.137
  118.2 0.3 fusion.4
  118.6 0.7 copy.104
  119.3 11.4 %all-to-all-start.2 = ((f32[1,32,448]{2,0,1:T(1,128)}), f32[1,32,448]{2,0,1:T(1,128)S(1)}, u32[]{:S(2)}, u32[]{:S(2)}) async-start(f32[1,32,448]{2,0,1:T(1,128)} %copy.104), calls=%async_computation.2 | async-start | bytes 131072 | tf_op jit(solution)/shard_map/all_to_all | solution.py:25
  130.7 7.8 %all-to-all-done.2 = f32[1,32,448]{2,0,1:T(1,128)S(1)} async-done(((f32[1,32,448]{2,0,1:T(1,128)}), f32[1,32,448]{2,0,1:T(1,128)S(1)}, u32[]{:S(2)}, u32[]{:S(2)}) %all-to-all-start.2) | async-done | bytes 57376 | tf_op jit(solution)/shard_map/all_to_all | solution.py:25
  138.5 0.2 reduce
  139.5 0.2 fusion.24
  139.7 7.0 %psum.28 = f32[16,64]{1,0:T(8,128)S(1)} all-reduce(f32[16,64]{1,0:T(8,128)S(1)} %fusion.24), channel_id=1, replica_groups=mesh['pencil_0'=4,'pencil_1'=4,'band_0'=8,'band_1'=2] {'pencil_0'}, use_global_device_ids=true, to_apply=%region_1.2 | all-reduce | flops 1024 | bytes 8192 | tf_op jit(solution)/shard_map/psum | solution.py:33
  146.7 7.0 %psum.29 = f32[16,64]{1,0:T(8,128)S(1)} all-reduce(f32[16,64]{1,0:T(8,128)S(1)} %psum.28), channel_id=1, replica_groups=mesh['pencil_0'=4,'pencil_1'=4,'band_0'=8,'band_1'=2] {'pencil_1'}, use_global_device_ids=true, to_apply=%region_2.3 | all-reduce | flops 1024 | bytes 8192 | tf_op jit(solution)/shard_map/psum | solution.py:33
  153.7 11.5 %psum.30 = f32[16,64]{1,0:T(8,128)S(1)} all-reduce(f32[16,64]{1,0:T(8,128)S(1)} %psum.29), channel_id=1, replica_groups=mesh['pencil_0'=4,'pencil_1'=4,'band_0'=8,'band_1'=2] {'band_0'}, use_global_device_ids=true, to_apply=%region_3.4 | all-reduce | flops 1024 | bytes 8192 | tf_op jit(solution)/shard_map/psum | solution.py:33
  165.2 9.9 %psum.31 = f32[16,64]{1,0:T(8,128)S(1)} all-reduce(f32[16,64]{1,0:T(8,128)S(1)} %psum.30), channel_id=1, replica_groups=mesh['pencil_0'=4,'pencil_1'=4,'band_0'=8,'band_1'=2] {'band_1'}, use_global_device_ids=true, to_apply=%region_4.5 | all-reduce | flops 1024 | bytes 8192 | tf_op jit(solution)/shard_map/psum | solution.py:33
  175.5 0.1 fusion.77
  175.6 0.1 fusion.60
  175.8 0.2 convolution_subtract_fusion.4
  176.0 0.2 fusion.80
  176.2 0.2 convolution_add_fusion.4
  176.4 0.2 convolution_subtract_fusion.2
  176.6 0.2 fusion.75
  176.8 0.2 convolution_add_fusion.3
  177.0 0.2 fusion.70
  177.2 0.2 fusion.68
  177.4 0.2 fusion.13
  177.6 0.2 fusion.12
  177.8 0.7 gather_fusion.2
  178.5 0.7 gather_fusion.1
  179.4 0.1 fusion.72
  179.5 0.2 fusion.11
  179.8 0.2 fusion.10
  180.1 0.3 fusion.66
  180.4 0.1 fusion.6
  180.5 0.3 fusion.8
  180.8 0.2 fusion.37
  181.2 0.2 fusion.41
  181.6 12.1 %all_to_all.57 = f32[16,2,448]{2,1,0:T(2,128)S(1)} all-to-all(f32[16,2,448]{2,1,0:T(2,128)S(1)} %pad_maximum_fusion.10), channel_id=1, replica_groups=mesh['pencil_0'=4,'pencil_1'=4,'band_0'=8,'band_1'=2] {'band_0','band_1'}, dimensions={0} | all-to-all | bytes 114688 | tf_op jit(solution)/shard_map/all_to_all | solution.py:25
  193.8 0.7 fusion.126
  (50 shorter events, 3.1 us)
Async XLA Ops:
  3.4 14.1 %all-to-all-start = ((f32[16,1,448]{2,1,0:T(1,128)}), f32[16,1,448]{2,1,0:T(1,128)S(1)}, u32[]{:S(2)}, u32[]{:S(2)}) async-start(f32[16,1,448]{2,1,0:T(1,128)} %reshape.237), calls=%async_computation | async-start | bytes 65536 | tf_op jit(solution)/shard_map/all_to_all | solution.py:127
  82.5 35.7 %copy-start.1 = (f32[1,32,224]{2,1,0:T(8,128)S(1)}, f32[1,32,224]{2,1,0:T(8,128)}, u32[]{:S(2)}) copy-start(f32[1,32,224]{2,1,0:T(8,128)} %param.4) | copy-start | bytes 86020
  84.1 91.1 %copy-start = (f32[2,16,16]{2,1,0:T(8,128)S(1)}, f32[2,16,16]{2,1,0:T(8,128)}, u32[]{:S(2)}) copy-start(f32[2,16,16]{2,1,0:T(8,128)} %param.7) | copy-start | bytes 6148
  106.1 10.3 %all-to-all-start.1 = ((f32[16,1,448]{2,1,0:T(1,128)}), f32[16,1,448]{2,1,0:T(1,128)S(1)}, u32[]{:S(2)}, u32[]{:S(2)}) async-start(f32[16,1,448]{2,1,0:T(1,128)} %reshape.239), calls=%async_computation.1 | async-start | bytes 65536 | tf_op jit(solution)/shard_map/all_to_all | solution.py:138
  119.3 19.2 %all-to-all-start.2 = ((f32[1,32,448]{2,0,1:T(1,128)}), f32[1,32,448]{2,0,1:T(1,128)S(1)}, u32[]{:S(2)}, u32[]{:S(2)}) async-start(f32[1,32,448]{2,0,1:T(1,128)} %copy.104), calls=%async_computation.2 | async-start | bytes 131072 | tf_op jit(solution)/shard_map/all_to_all | solution.py:25
  179.2 15.3 %copy-start.2 = (f32[16]{0:T(128)}, f32[16]{0:T(128)S(1)}, u32[]{:S(2)}) copy-start(f32[16]{0:T(128)S(1)} %div.48) | copy-start | bytes 196
where the time goes:
time: 196 us; the launch traced here: 194 us
  local copies, waits for them, and re-layouts  90.3 us (46%)
  blocking collectives  47.5 us (24%)
  starting transfers between devices  22.8 us (12%)
  waiting for transfers between devices  16.7 us (9%)
  matrix products  11.5 us (6%)
  other arithmetic  4.74 us (2%)
    scatter x1, local copies, waits for them, and re-layouts, shards(): planes = planes.at[:, :, :, columns].set(received)  47.1 us
    psum x4, blocking collectives, one_axis_at_a_time(): return functools.reduce(lax.psum, axes, x)  35.4 us
    all_to_all x1, blocking collectives, sent_together(): lax.all_to_all(both, axis, split_axis=split_dim, concat_axis=concat_dim,...  12.1 us
    all_to_all x1, starting transfers between devices, sent_together(): lax.all_to_all(both, axis, split_axis=split_dim, concat_axis=concat_dim,...  11.4 us
    another operation x1, local copies, waits for them, and re-layouts  11.2 us
    reshape x1, local copies, waits for them, and re-layouts, shards(): planes.reshape(row_count, 2, planes_dev, grid_size * grid_size)  9.43 us
    all_to_all x1, waiting for transfers between devices, sent_together(): lax.all_to_all(both, axis, split_axis=split_dim, concat_axis=concat_dim,...  7.8 us
    all_to_all x1, starting transfers between devices, shards(): lax.all_to_all(zsticks, PENCIL, split_axis=2, concat_axis=3, tiled=True)  7.58 us
  transfers between devices with their start and end apart: 3, of which 3 were waited for; matrix products, arithmetic and copies ran while one was open for 2% of the time, Pallas kernels for 0%

commit v1 on v0

v1 whole, which is shorter than its diff:
```python
import functools

import jax
import jax.numpy as jnp
import ml_dtypes
import numpy as np
from jax import lax
from jax.experimental import pallas as pl
from jax.experimental.pallas import tpu as pltpu
from jax.sharding import PartitionSpec as P

GRID = 112
BANDS = 16
PENCILS = 16
PLANES = 7
STICKS = 512
OWN = 32
RADIUS = 28

f32 = jnp.float32
bf16 = jnp.bfloat16
MESH = pl.DeviceIdType.MESH
NN = (((1,), (0,)), ((), ()))
NT = (((1,), (1,)), ((), ()))


def parts_of(table, count):
    parts = []
    for _ in range(count):
        part = table.astype(ml_dtypes.bfloat16)
        parts.append(part)
        table = table - part.astype(np.float64)
    return np.stack(parts)


def wave_table():
    index = np.arange(GRID)
    angle = 2.0 * np.pi * (np.outer(index, index) % GRID) / GRID
    table = np.zeros((256, 128))
    table[:GRID, :GRID] = np.cos(angle)
    table[128 : 128 + GRID, :GRID] = np.sin(angle)
    return parts_of(table, 3)


def z_tables():
    inverse = np.zeros((64, 4, 256))
    forward = np.zeros((64, 4, 256))
    k = np.arange(GRID)
    for p in range(PENCILS):
        for r in range(4):
            for q in range(4):
                z = 4 * (q % 2) + r
                if z >= PLANES:
                    continue
                angle = 2.0 * np.pi * ((k * (PLANES * p + z)) % GRID) / GRID
                cosine, sine = np.cos(angle), np.sin(angle)
                real = q // 2 == 0
                row = 4 * p + r
                inverse[row, q, :GRID] = cosine if real else sine
                inverse[row, q, 128 : 128 + GRID] = -sine if real else cosine
                forward[row, q, :GRID] = cosine if real else sine
                forward[row, q, 128 : 128 + GRID] = -sine if real else cosine
    return parts_of(inverse.reshape(64, 1024), 2), parts_of(forward.reshape(64, 1024) / float(GRID) ** 3, 2)


def split(x):
    high = x.astype(bf16)
    return high, (x - high.astype(f32)).astype(bf16)


def dot(a, b, dims=NN):
    return lax.dot_general(a, b, dims, preferred_element_type=f32)


def dot3(a, b, dims=NN):
    return dot(a[0], b[0], dims) + dot(a[0], b[1], dims) + dot(a[1], b[0], dims)


def dot_exact(a, b, dims=NN):
    return lax.dot_general(a, b, dims, precision=lax.Precision.HIGHEST, preferred_element_type=f32)


def slot_of(p):
    return lax.rem(p, 4) * 4 + lax.div(p, 4)


def frequency(index):
    return jnp.where(index < GRID // 2, index, index - GRID).astype(f32)


def wide(x):
    lane = lax.broadcasted_iota(jnp.int32, x.shape, 1)
    moved = pltpu.roll(x, 16, 1)
    return jnp.where(lane < GRID, x, jnp.where(lane < 128, 0.0, moved))


def narrow(x):
    lane = lax.broadcasted_iota(jnp.int32, x.shape, 1)
    moved = pltpu.roll(x, 240, 1)
    return jnp.where(lane < GRID, x, moved)


def turned(x):
    return jnp.concatenate([x[:, 128:], -x[:, :128]], axis=1)


def kernel(
    coeffs_ref, columns_ref, potential_ref, ritz_ref, inverse_ref, forward_ref, wave_ref,
    refined_ref, refined_h_ref, values_ref,
    pad_ref, own_ref, block_ref, send_b, recv_b, send_d, recv_d, psi_ref, a_ref, t_ref, v_ref, p_ref, c_ref,
    bands_ref, own_h_ref, bands_h_ref, sums_ref, send_g, recv_g, row_ref, recv_r,
    sem_sb, sem_rb, sem_sd, sem_rd, sem_sp, sem_rp, sem_sh, sem_rh, sem_sg, sem_rg, sem_sr, sem_rr,
):
    pencil = lax.axis_index("pencil")
    band = lax.axis_index("band")

    def pencil_peer(d):
        return lax.rem(pencil + d, PENCILS)

    def band_peer(d):
        return lax.rem(band + d, BANDS)

    def each(body):
        def step(d, carry):
            body(d)
            return carry

        lax.fori_loop(1, 16, step, 0)

    def to_b(p, mine):
        return pltpu.make_async_remote_copy(
            send_b.at[p], recv_b.at[slot_of(mine)], sem_sb.at[p], sem_rb.at[mine],
            device_id=(p, band), device_id_type=MESH,
        )

    def to_d(p, mine):
        return pltpu.make_async_remote_copy(
            send_d.at[slot_of(p)], recv_d.at[mine], sem_sd.at[p], sem_rd.at[mine],
            device_id=(p, band), device_id_type=MESH,
        )

    def to_g(p, mine):
        return pltpu.make_async_remote_copy(
            send_g, recv_g.at[mine], sem_sg.at[p], sem_rg.at[mine], device_id=(p, band), device_id_type=MESH
        )

    def to_p(b, mine):
        return pltpu.make_async_remote_copy(
            own_ref, bands_ref.at[mine], sem_sp.at[b], sem_rp.at[mine], device_id=(pencil, b), device_id_type=MESH
        )

    def to_h(b, mine):
        return pltpu.make_async_remote_copy(
            own_h_ref, bands_h_ref.at[mine], sem_sh.at[b], sem_rh.at[mine], device_id=(pencil, b), device_id_type=MESH
        )

    def to_r(b, mine):
        return pltpu.make_async_remote_copy(
            row_ref, recv_r.at[mine], sem_sr.at[b], sem_rr.at[mine], device_id=(pencil, b), device_id_type=MESH
        )

    barrier = pltpu.get_barrier_semaphore()

    def greet(d):
        pl.semaphore_signal(barrier, inc=1, device_id=(pencil_peer(d), band), device_id_type=MESH)
        pl.semaphore_signal(barrier, inc=1, device_id=(pencil, band_peer(d)), device_id_type=MESH)

    each(greet)

    pad_ref[...] = jnp.zeros_like(pad_ref)
    pad_ref[:, : 2 * GRID] = coeffs_ref[0]
    own = wide(pad_ref[...])
    own_ref[...] = own
    own_high, own_low = split(own)
    block_ref[...] = jnp.zeros_like(block_ref)
    for q in range(4):
        block_ref[0, 32 * q : 32 * q + 32, 256 * q : 256 * q + 256] = own_high
        block_ref[1, 32 * q : 32 * q + 32, 256 * q : 256 * q + 256] = own_low
    packed = dot3((inverse_ref[0], inverse_ref[1]), (block_ref[0], block_ref[1]), NT)
    send_b[...] = packed.reshape(PENCILS, 4, 128)

    pl.semaphore_wait(barrier, 30)
    each(lambda d: to_b(pencil_peer(d), pencil).start())
    each(lambda d: to_p(band_peer(d), band).start())
    recv_b[slot_of(pencil)] = send_b[pencil]
    bands_ref[band] = own

    columns = columns_ref[...]
    index_x = lax.div(columns, GRID)
    index_y = lax.rem(columns, GRID)
    row = lax.broadcasted_iota(jnp.int32, (128, STICKS), 0)
    hot_x = jnp.where(row == index_x, 1.0, 0.0).astype(bf16)
    hot_y = jnp.where(row == index_y, 1.0, 0.0).astype(bf16)
    a_ref[...] = dot(wave_ref[0], hot_x) + dot(wave_ref[1], hot_x) + dot(wave_ref[2], hot_x)
    for part in range(2):
        table = dot(wave_ref[part], hot_y).astype(bf16)
        t_ref[part, :, :STICKS] = table
        t_ref[part, :128, STICKS:] = -table[128:]
        t_ref[part, 128:, STICKS:] = table[:128]
    v_ref[...] = jnp.zeros_like(v_ref)

    def lay_out(g, carry):
        block = potential_ref[:, pl.ds(pl.multiple_of(896 * g, 128), 896)]
        for k in range(8):
            v_ref[8 * g + k, :PLANES, :GRID] = block[:, GRID * k : GRID * k + GRID]
        return carry

    lax.fori_loop(0, 14, lay_out, 0)

    freq_x, freq_y = frequency(index_x), frequency(index_y)
    lateral = freq_x * freq_x + freq_y * freq_y
    stick = lax.broadcasted_iota(jnp.int32, (OWN, STICKS), 1)
    mine = stick == lax.broadcasted_iota(jnp.int32, (OWN, STICKS), 0) + OWN * pencil
    own_lateral = jnp.sum(jnp.where(mine, lateral, 0.0), axis=1, keepdims=True)
    lane = lax.broadcasted_iota(jnp.int32, (OWN, 256), 1)
    freq_z = frequency(jnp.where(lane < 128, lane, lane - 128))
    kinetic = 0.5 * (own_lateral + freq_z * freq_z) / float(RADIUS * RADIUS)

    each(lambda d: to_b(pencil_peer(d), pencil_peer(d)).wait_recv())
    got = recv_b[...].reshape(4, 16, 128)
    group = lax.div(lax.broadcasted_iota(jnp.int32, (16, 128), 1), 32)
    for q in range(4):
        out = got[0] if q == 0 else pltpu.roll(got[0], (-32 * q) % 128, 1)
        for p in range(1, 4):
            moved = got[p] if p == q else pltpu.roll(got[p], (32 * (p - q)) % 128, 1)
            out = jnp.where(group == p, moved, out)
        for t in range(4):
            psi_ref[q // 2, 4 * (q % 2) : 4 * (q % 2) + 4, 128 * t : 128 * t + 128] = out[4 * t : 4 * t + 4]

    psi_r, psi_i = psi_ref[0], psi_ref[1]

    def phases(x):
        return a_ref[pl.ds(x, 1), :], a_ref[pl.ds(128 + x, 1), :]

    def spread(n, carry):
        real, imag = [], []
        for k in range(2):
            a_r, a_i = phases(2 * n + k)
            real.append(a_r * psi_r - a_i * psi_i)
            imag.append(a_r * psi_i + a_i * psi_r)
        rows = pl.ds(pl.multiple_of(16 * n, 16), 16)
        p_ref[0, rows, :STICKS], p_ref[1, rows, :STICKS] = split(jnp.concatenate(real, axis=0))
        p_ref[0, rows, STICKS:], p_ref[1, rows, STICKS:] = split(jnp.concatenate(imag, axis=0))
        return carry

    lax.fori_loop(0, 56, spread, 0)

    def plane_rows(n, carry):
        rows = pl.ds(pl.multiple_of(224 * n, 224), 224)
        u = dot3((p_ref[0, rows, :], p_ref[1, rows, :]), (t_ref[0], t_ref[1]), NT)
        v = v_ref[pl.ds(28 * n, 28)].reshape(224, 128)
        w = u * jnp.concatenate([v, v], axis=1)
        c_ref[rows, :] = dot3(split(w), (t_ref[0], t_ref[1]))
        return carry

    lax.fori_loop(0, 4, plane_rows, 0)

    def collect(n, carry):
        w_r, w_i = carry
        for k in range(4):
            x = 4 * n + k
            a_r, a_i = phases(x)
            rows = pl.ds(pl.multiple_of(8 * x, 8), 8)
            c_r, c_i = c_ref[rows, :STICKS], c_ref[rows, STICKS:]
            w_r = w_r + (a_r * c_r + a_i * c_i)
            w_i = w_i + (a_r * c_i - a_i * c_r)
        return w_r, w_i

    zero = jnp.zeros((8, STICKS), f32)
    sums = lax.fori_loop(0, 28, collect, (zero, zero))

    outs = []
    for q in range(4):
        half = sums[q // 2][4 * (q % 2) : 4 * (q % 2) + 4]
        outs.append(jnp.concatenate([half[:, 128 * t : 128 * t + 128] for t in range(4)], axis=0))
    for p in range(4):
        out = outs[0] if p == 0 else pltpu.roll(outs[0], (-32 * p) % 128, 1)
        for q in range(1, 4):
            moved = outs[q] if p == q else pltpu.roll(outs[q], (32 * (q - p)) % 128, 1)
            out = jnp.where(group == q, moved, out)
        send_d[4 * p : 4 * p + 4] = out.reshape(4, 4, 128)
    each(lambda d: to_d(pencil_peer(d), pencil).start())
    recv_d[pencil] = send_d[slot_of(pencil)]

    pick = lax.broadcasted_iota(jnp.int32, (256, 128), 0)
    ones = jnp.ones((8, 256), f32)

    def gram_row(values, first):
        other = turned(values)

        def one(i, carry):
            member = bands_ref[i]
            real, imag = member * values, member * other
            rows = pl.ds(pl.multiple_of(8 * i, 8), 8)
            later = pl.ds(pl.multiple_of(128 + 8 * i, 8), 8)
            sums_ref[rows, :] = (real[:8] + real[8:16]) + (real[16:24] + real[24:])
            sums_ref[later, :] = (imag[:8] + imag[8:16]) + (imag[16:24] + imag[24:])
            return carry

        lax.fori_loop(0, BANDS, one, 0)
        target = lax.broadcasted_iota(jnp.int32, (256, 128), 1)
        chosen = jnp.where(lax.div(pick, 8) + first == target, 1.0, 0.0)
        return dot_exact(dot_exact(ones, sums_ref[...], NT), chosen)[:1]

    each(lambda d: to_p(band_peer(d), band_peer(d)).wait_recv())
    overlap_row = gram_row(own, 32)

    each(lambda d: to_d(pencil_peer(d), pencil_peer(d)).wait_recv())
    back = split(recv_d[...].reshape(64, 128).T)
    own_h = kinetic * own
    for q in range(4):
        rows, cols = slice(32 * q, 32 * q + 32), slice(256 * q, 256 * q + 256)
        own_h = own_h + dot3(
            (back[0][rows], back[1][rows]), (forward_ref[0, :, cols], forward_ref[1, :, cols])
        )
    own_h_ref[...] = own_h
    each(lambda d: to_h(band_peer(d), band).start())
    bands_h_ref[band] = own_h

    send_g[...] = gram_row(own_h, 0) + overlap_row
    each(lambda d: to_g(pencil_peer(d), pencil).start())
    recv_g[pencil] = send_g[...]
    each(lambda d: to_g(pencil_peer(d), pencil_peer(d)).wait_recv())
    row_ref[...] = jnp.sum(recv_g[...], axis=0) / float(STICKS * GRID)
    each(lambda d: to_r(band_peer(d), band).start())
    recv_r[band] = row_ref[...]

    x_r, x_i = ritz_ref[0], ritz_ref[1]
    xt = jnp.concatenate([x_r.T, x_i.T], axis=1)
    conj = jnp.concatenate(
        [jnp.concatenate([x_r, -x_i], axis=1), jnp.concatenate([x_i, x_r], axis=1)], axis=0
    )
    each(lambda d: to_r(band_peer(d), band_peer(d)).wait_recv())
    grams = recv_r[...].reshape(BANDS, 128)
    lane = lax.broadcasted_iota(jnp.int32, (BANDS, 128), 1)
    swapped = jnp.where(lax.rem(lane, 32) < 16, -pltpu.roll(grams, 112, 1), pltpu.roll(grams, 16, 1))
    half = dot_exact(xt, jnp.concatenate([grams, swapped], axis=0))
    energy = dot_exact(half[:, :32], conj)
    metric = dot_exact(half[:, 32:64], conj)
    row16 = lax.broadcasted_iota(jnp.int32, (BANDS, 16), 0)
    diagonal = row16 == lax.broadcasted_iota(jnp.int32, (BANDS, 16), 1)
    ratio = jnp.where(diagonal, energy[:, :16] / metric[:, :16], 0.0)
    value_j = jnp.sum(ratio, axis=1, keepdims=True)
    value_i = jnp.sum(ratio, axis=0, keepdims=True)
    values_ref[...] = value_i
    spacing = value_j - value_i
    factor = spacing / jnp.maximum(spacing * spacing, (0.25 / BANDS) ** 2)
    residual_r = jnp.where(diagonal, 1.0, 0.0) - metric[:, :16]
    residual_i = -metric[:, 16:]
    update_r = jnp.where(diagonal, 0.5 * residual_r, (energy[:, :16] + value_j * residual_r) * factor)
    update_i = jnp.where(diagonal, 0.5 * residual_i, (energy[:, 16:] + value_j * residual_i) * factor)
    chosen = row16 == band
    u_r = jnp.sum(jnp.where(chosen, update_r + jnp.where(diagonal, 1.0, 0.0), 0.0), axis=0, keepdims=True)
    u_i = jnp.sum(jnp.where(chosen, update_i, 0.0), axis=0, keepdims=True)
    new_r = jnp.sum(x_r * u_r - x_i * u_i, axis=1, keepdims=True)
    new_i = jnp.sum(x_r * u_i + x_i * u_r, axis=1, keepdims=True)

    def rotate(members):
        along = jnp.zeros((OWN, 256), f32)
        across = jnp.zeros((OWN, 256), f32)
        for i in range(BANDS):
            member = members[i]
            along = along + new_r[i : i + 1] * member
            across = across + new_i[i : i + 1] * member
        return narrow(along - turned(across))[:, : 2 * GRID]

    refined_ref[0] = rotate(bands_ref)
    each(lambda d: to_h(band_peer(d), band_peer(d)).wait_recv())
    refined_h_ref[0] = rotate(bands_h_ref)

    def finish(d):
        to_b(pencil_peer(d), pencil).wait_send()
        to_d(pencil_peer(d), pencil).wait_send()
        to_g(pencil_peer(d), pencil).wait_send()
        to_p(band_peer(d), band).wait_send()
        to_h(band_peer(d), band).wait_send()
        to_r(band_peer(d), band).wait_send()

    each(finish)


def shards(coeffs, columns, potential, ritz_vectors):
    inverse, forward = z_tables()
    vmem = pl.BlockSpec(memory_space=pltpu.VMEM)
    refined, refined_h, values = pl.pallas_call(
        kernel,
        out_shape=(
            jax.ShapeDtypeStruct((1, OWN, 2 * GRID), f32),
            jax.ShapeDtypeStruct((1, OWN, 2 * GRID), f32),
            jax.ShapeDtypeStruct((1, BANDS), f32),
        ),
        in_specs=[vmem] * 7,
        out_specs=(vmem,) * 3,
        scratch_shapes=[
            pltpu.VMEM((OWN, 256), f32),
            pltpu.VMEM((OWN, 256), f32),
            pltpu.VMEM((2, 128, 1024), bf16),
            pltpu.VMEM((16, 4, 128), f32),
            pltpu.VMEM((16, 4, 128), f32),
            pltpu.VMEM((16, 4, 128), f32),
            pltpu.VMEM((16, 4, 128), f32),
            pltpu.VMEM((2, 8, STICKS), f32),
            pltpu.VMEM((256, STICKS), f32),
            pltpu.VMEM((2, 256, 1024), bf16),
            pltpu.VMEM((GRID, 8, 128), f32),
            pltpu.VMEM((2, 896, 1024), bf16),
            pltpu.VMEM((896, 1024), f32),
            pltpu.VMEM((BANDS, OWN, 256), f32),
            pltpu.VMEM((OWN, 256), f32),
            pltpu.VMEM((BANDS, OWN, 256), f32),
            pltpu.VMEM((256, 256), f32),
            pltpu.VMEM((1, 128), f32),
            pltpu.VMEM((16, 1, 128), f32),
            pltpu.VMEM((1, 128), f32),
            pltpu.VMEM((16, 1, 128), f32),
        ]
        + [pltpu.SemaphoreType.DMA((16,))] * 12,
        compiler_params=pltpu.CompilerParams(
            collective_id=0, has_side_effects=True, vmem_limit_bytes=48 * 2**20
        ),
    )(
        coeffs,
        columns.reshape(1, STICKS),
        potential,
        ritz_vectors,
        jnp.asarray(inverse),
        jnp.asarray(forward),
        jnp.asarray(wave_table()),
    )
    return refined, refined_h, values.reshape(BANDS)


def solution(mesh):
    return jax.shard_map(
        shards,
        mesh=mesh,
        in_specs=(P("band", "pencil", None), P(), P("pencil", None), P()),
        out_specs=(P("band", "pencil", None), P("band", "pencil", None), P()),
        check_vma=False,
    )
```

time: 196 us -> 53.6 us (0.27)
  local copies, waits for them, and re-layouts: 90.3 us -> 7.71 us
  blocking collectives: 47.5 us -> 0 us
  Pallas kernels: 0 us -> 44.9 us
  starting transfers between devices: 22.8 us -> 0 us
  waiting for transfers between devices: 16.7 us -> 0 us
  matrix products: 11.5 us -> 0 us
  other arithmetic: 4.74 us -> 0 us
    scatter x1 -> x0, local copies, waits for them, and re-layouts: 47.1 us -> none  [shards(): planes = planes.at[:, :, :, columns].set(received)]
    pallas_call x0 -> x1, Pallas kernels: none -> 44.9 us  [shards(): pl.pallas_call(kernel, out_shape=(jax.ShapeDtypeStruct((1, OWN, 2 * GRID)...]
    psum x4 -> x0, blocking collectives: 35.4 us -> none  [one_axis_at_a_time(): return functools.reduce(lax.psum, axes, x)]
    all_to_all x3 -> x0, starting transfers between devices: 22.8 us -> none  [the longest x1 11.4 us: sent_together(): lax.all_to_all(both, axis, split_axis=split_dim, concat_axis=concat_dim,...]
    all_to_all x3 -> x0, waiting for transfers between devices: 16.7 us -> none  [the longest x1 7.8 us: sent_together(): lax.all_to_all(both, axis, split_axis=split_dim, concat_axis=concat_dim,...]
    all_to_all x1 -> x0, blocking collectives: 12.1 us -> none  [sent_together(): lax.all_to_all(both, axis, split_axis=split_dim, concat_axis=concat_dim,...]
    dot_general x29 -> x0, matrix products: 11.5 us -> none  [the longest x1 1.61 us: shards(): planes = jnp.einsum('bczxy,cxdu->bdzuy', planes, forward, precision=precise)]
    another operation x1 -> x0, local copies, waits for them, and re-layouts: 11.2 us -> none
  transfers between devices with their start and end apart: 3 -> 0, of which waited for: 3 -> 0; matrix products, arithmetic and copies ran while one was open for 2% -> 0% of each run, Pallas kernels for 0% -> 0%
where the time goes in v1:
time: 53.6 us; the launch traced here: 53.3 us
  Pallas kernels  44.9 us (84%)
  local copies, waits for them, and re-layouts  7.71 us (14%)
  between operations  0.65 us (1%)
    pallas_call x1, Pallas kernels, shards(): pl.pallas_call(kernel, out_shape=(jax.ShapeDtypeStruct((1, OWN, 2 * GRID)...  44.9 us
    unnamed x17, local copies, waits for them, and re-layouts  7.71 us

profile of v1, /device:TPU:1, one launch (start us, length us, event | category | flops | bytes accessed | tf_op | source)
XLA Modules:
  0.0 53.3 jit_solution(1508988294108573432)
XLA Ops:
  0.6 0.0 copy-start
  0.6 1.0 %copy-done = f32[7,12544]{1,0:T(8,128)S(1)} copy-done((f32[7,12544]{1,0:T(8,128)S(1)}, f32[7,12544]{1,0:T(8,128)}, u32[]{:S(2)}) %copy-start) | copy-done | bytes 351256
  1.6 0.0 copy-start.1
  1.6 0.9 %copy-done.1 = bf16[2,64,1024]{2,1,0:T(8,128)(2,1)S(1)} copy-done((bf16[2,64,1024]{2,1,0:T(8,128)(2,1)S(1)}, bf16[2,64,1024]{2,1,0:T(8,128)(2,1)}, u32[]{:S(2)}) %copy-start.1) | copy-done | bytes 262168
  2.6 0.0 copy-start.2
  2.6 0.9 %copy-done.2 = bf16[2,64,1024]{2,1,0:T(8,128)(2,1)S(1)} copy-done((bf16[2,64,1024]{2,1,0:T(8,128)(2,1)S(1)}, bf16[2,64,1024]{2,1,0:T(8,128)(2,1)}, u32[]{:S(2)}) %copy-start.2) | copy-done | bytes 262168
  3.5 0.0 copy-start.3
  3.5 0.9 %copy-done.3 = bf16[3,256,128]{2,1,0:T(8,128)(2,1)S(1)} copy-done((bf16[3,256,128]{2,1,0:T(8,128)(2,1)S(1)}, bf16[3,256,128]{2,1,0:T(8,128)(2,1)}, u32[]{:S(2)}) %copy-start.3) | copy-done | bytes 196632
  4.5 0.0 copy-start.4
  4.5 0.8 %copy-done.4 = f32[1,32,224]{2,1,0:T(8,128)S(1)} copy-done((f32[1,32,224]{2,1,0:T(8,128)S(1)}, f32[1,32,224]{2,1,0:T(8,128)}, u32[]{:S(2)}) %copy-start.4) | copy-done | bytes 28696
  5.2 0.0 copy-start.5
  5.2 0.7 %copy-done.5 = f32[2,16,16]{2,1,0:T(8,128)S(1)} copy-done((f32[2,16,16]{2,1,0:T(8,128)S(1)}, f32[2,16,16]{2,1,0:T(8,128)}, u32[]{:S(2)}) %copy-start.5) | copy-done | bytes 2072
  5.9 0.0 copy-start.6
  5.9 0.7 %copy-done.6 = s32[512]{0:T(512)S(1)} copy-done((s32[512]{0:T(512)S(1)}, s32[512]{0:T(512)}, u32[]{:S(2)}) %copy-start.6) | copy-done | bytes 2072
  6.6 44.9 %shard_map.94 = (f32[1,32,224]{2,1,0:T(8,128)S(1)}, f32[1,32,224]{2,1,0:T(8,128)S(1)}, f32[1,16]{1,0:T(1,128)S(1)}) custom-call(f32[1,32,224]{2,1,0:T(8,128)S(1)} %copy-done.4, s32[1,512]{1,0:T(1,128)S(1)} %bitcast.2, f32[7,12544]{1,0:T(8,128)S(1)} %copy-done, f32[2,16,16]{2,1,0:T(8,128)S(1)} %copy-done.5, bf16[2,64,1024]{2,1,0:T(8,128)(2,1)S(1)} %copy-done.2, ...), custom_call_target="tpu_custom_call" | custom-call | tf_op jit(solution)/shard_map/pallas_call | solution.py:385
  51.5 0.6 %copy.13 = f32[1,32,224]{2,1,0:T(8,128)} copy(f32[1,32,224]{2,1,0:T(8,128)S(1)} %get-tuple-element.12) | data formatting | bytes 57344
  52.1 0.6 %copy.14 = f32[1,32,224]{2,1,0:T(8,128)} copy(f32[1,32,224]{2,1,0:T(8,128)S(1)} %get-tuple-element.13) | data formatting | bytes 57344
  52.8 0.5 copy.15
Async XLA Ops:
  0.6 1.0 %copy-start = (f32[7,12544]{1,0:T(8,128)S(1)}, f32[7,12544]{1,0:T(8,128)}, u32[]{:S(2)}) copy-start(f32[7,12544]{1,0:T(8,128)} %potential_ref.1) | copy-start | bytes 1053700
  1.6 0.9 %copy-start.1 = (bf16[2,64,1024]{2,1,0:T(8,128)(2,1)S(1)}, bf16[2,64,1024]{2,1,0:T(8,128)(2,1)}, u32[]{:S(2)}) copy-start(bf16[2,64,1024]{2,1,0:T(8,128)(2,1)} %constant.7.clone.forward_ref) | copy-start | bytes 786436
  2.6 0.9 %copy-start.2 = (bf16[2,64,1024]{2,1,0:T(8,128)(2,1)S(1)}, bf16[2,64,1024]{2,1,0:T(8,128)(2,1)}, u32[]{:S(2)}) copy-start(bf16[2,64,1024]{2,1,0:T(8,128)(2,1)} %constant.6.clone.inverse_ref) | copy-start | bytes 786436
  3.5 0.9 %copy-start.3 = (bf16[3,256,128]{2,1,0:T(8,128)(2,1)S(1)}, bf16[3,256,128]{2,1,0:T(8,128)(2,1)}, u32[]{:S(2)}) copy-start(bf16[3,256,128]{2,1,0:T(8,128)(2,1)} %constant.8.clone.wave_ref) | copy-start | bytes 589828
  4.5 0.8 %copy-start.4 = (f32[1,32,224]{2,1,0:T(8,128)S(1)}, f32[1,32,224]{2,1,0:T(8,128)}, u32[]{:S(2)}) copy-start(f32[1,32,224]{2,1,0:T(8,128)} %coeffs_ref.1) | copy-start | bytes 86020
  5.2 0.7 %copy-start.5 = (f32[2,16,16]{2,1,0:T(8,128)S(1)}, f32[2,16,16]{2,1,0:T(8,128)}, u32[]{:S(2)}) copy-start(f32[2,16,16]{2,1,0:T(8,128)} %ritz_ref.1) | copy-start | bytes 6148
  5.9 0.7 %copy-start.6 = (s32[512]{0:T(512)S(1)}, s32[512]{0:T(512)}, u32[]{:S(2)}) copy-start(s32[512]{0:T(512)} %param.8) | copy-start | bytes 6148

commit v2 on v1

--- a/solution.py
+++ b/solution.py
@@ -105,11 +105,12 @@
 
 
 def kernel(
-    coeffs_ref, columns_ref, potential_ref, ritz_ref, inverse_ref, forward_ref, wave_ref,
+    coeffs_hbm, columns_hbm, potential_hbm, ritz_hbm, inverse_hbm, forward_hbm, wave_hbm,
     refined_ref, refined_h_ref, values_ref,
-    pad_ref, own_ref, block_ref, send_b, recv_b, send_d, recv_d, psi_ref, a_ref, t_ref, v_ref, p_ref, c_ref,
-    bands_ref, own_h_ref, bands_h_ref, sums_ref, send_g, recv_g, row_ref, recv_r,
-    sem_sb, sem_rb, sem_sd, sem_rd, sem_sp, sem_rp, sem_sh, sem_rh, sem_sg, sem_rg, sem_sr, sem_rr,
+    coeffs_ref, columns_ref, potential_ref, ritz_ref, inverse_ref, forward_ref, wave_ref, sem_in,
+    pad_ref, block_ref, send_b, recv_b, send_d, recv_d, psi_ref, a_ref, t_ref, v_ref, p_ref, w_ref, c_ref,
+    bands_ref, bands_h_ref, sums_ref, send_g, recv_g, row_ref, recv_r,
+    sem_sb, sem_rb, sem_sd, sem_rd, sem_sp, sem_fp, sem_rp, sem_sh, sem_fh, sem_rh, sem_sg, sem_rg, sem_sr, sem_rr,
 ):
     pencil = lax.axis_index("pencil")
     band = lax.axis_index("band")
@@ -144,33 +145,68 @@
             send_g, recv_g.at[mine], sem_sg.at[p], sem_rg.at[mine], device_id=(p, band), device_id_type=MESH
         )
 
+    sibling = band + 1 - 2 * lax.rem(band, 2)
+
+    def chip_peer(d):
+        return lax.rem(band + 2 * d, BANDS)
+
     def to_p(b, mine):
         return pltpu.make_async_remote_copy(
-            own_ref, bands_ref.at[mine], sem_sp.at[b], sem_rp.at[mine], device_id=(pencil, b), device_id_type=MESH
+            bands_ref.at[mine], bands_ref.at[mine], sem_sp.at[b], sem_rp.at[mine],
+            device_id=(pencil, b), device_id_type=MESH,
+        )
+
+    def hand_p(q):
+        return pltpu.make_async_remote_copy(
+            bands_ref.at[q], bands_ref.at[q], sem_fp.at[q], sem_rp.at[q],
+            device_id=(pencil, sibling), device_id_type=MESH,
         )
 
     def to_h(b, mine):
         return pltpu.make_async_remote_copy(
-            own_h_ref, bands_h_ref.at[mine], sem_sh.at[b], sem_rh.at[mine], device_id=(pencil, b), device_id_type=MESH
-        )
+            bands_h_ref.at[mine], bands_h_ref.at[mine], sem_sh.at[b], sem_rh.at[mine],
+            device_id=(pencil, b), device_id_type=MESH,
+        )
+
+    def hand_h(q):
+        return pltpu.make_async_remote_copy(
+            bands_h_ref.at[q], bands_h_ref.at[q], sem_fh.at[q], sem_rh.at[q],
+            device_id=(pencil, sibling), device_id_type=MESH,
+        )
+
+    def chips(body, first=1):
+        def step(d, carry):
+            body(d)
+            return carry
+
+        lax.fori_loop(first, 8, step, 0)
 
     def to_r(b, mine):
         return pltpu.make_async_remote_copy(
             row_ref, recv_r.at[mine], sem_sr.at[b], sem_rr.at[mine], device_id=(pencil, b), device_id_type=MESH
         )
 
+    sources = (coeffs_hbm, inverse_hbm, columns_hbm, wave_hbm, potential_hbm, forward_hbm, ritz_hbm)
+    targets = (coeffs_ref, inverse_ref, columns_ref, wave_ref, potential_ref, forward_ref, ritz_ref)
+    loads = [pltpu.make_async_copy(a, b, sem_in.at[k]) for k, (a, b) in enumerate(zip(sources, targets))]
     barrier = pltpu.get_barrier_semaphore()
+    for load in loads[:2]:
+        load.start()
 
     def greet(d):
         pl.semaphore_signal(barrier, inc=1, device_id=(pencil_peer(d), band), device_id_type=MESH)
         pl.semaphore_signal(barrier, inc=1, device_id=(pencil, band_peer(d)), device_id_type=MESH)
 
     each(greet)
+    for load in loads[2:]:
+        load.start()
+    for load in loads[:2]:
+        load.wait()
 
     pad_ref[...] = jnp.zeros_like(pad_ref)
     pad_ref[:, : 2 * GRID] = coeffs_ref[0]
     own = wide(pad_ref[...])
-    own_ref[...] = own
+    bands_ref[band] = own
     own_high, own_low = split(own)
     block_ref[...] = jnp.zeros_like(block_ref)
     for q in range(4):
@@ -181,9 +217,11 @@
 
     pl.semaphore_wait(barrier, 30)
     each(lambda d: to_b(pencil_peer(d), pencil).start())
-    each(lambda d: to_p(band_peer(d), band).start())
+    chips(lambda d: to_p(chip_peer(d), band).start())
+    hand_p(band).start()
     recv_b[slot_of(pencil)] = send_b[pencil]
-    bands_ref[band] = own
+    for load in loads[2:]:
+        load.wait()
 
     columns = columns_ref[...]
     index_x = lax.div(columns, GRID)
@@ -245,15 +283,18 @@
 
     lax.fori_loop(0, 56, spread, 0)
 
-    def plane_rows(n, carry):
-        rows = pl.ds(pl.multiple_of(224 * n, 224), 224)
-        u = dot3((p_ref[0, rows, :], p_ref[1, rows, :]), (t_ref[0], t_ref[1]), NT)
-        v = v_ref[pl.ds(28 * n, 28)].reshape(224, 128)
-        w = u * jnp.concatenate([v, v], axis=1)
-        c_ref[rows, :] = dot3(split(w), (t_ref[0], t_ref[1]))
+    u = dot3((p_ref[0], p_ref[1]), (t_ref[0], t_ref[1]), NT)
+    v = v_ref[...].reshape(896, 128)
+    for part in range(2):
+        cols = slice(128 * part, 128 * part + 128)
+        w_ref[0, :, cols], w_ref[1, :, cols] = split(u[:, cols] * v)
+
+    def back_rows(n, carry):
+        rows = pl.ds(pl.multiple_of(448 * n, 448), 448)
+        c_ref[rows, :] = dot3((w_ref[0, rows, :], w_ref[1, rows, :]), (t_ref[0], t_ref[1]))
         return carry
 
-    lax.fori_loop(0, 4, plane_rows, 0)
+    lax.fori_loop(0, 2, back_rows, 0)
 
     def collect(n, carry):
         w_r, w_i = carry
@@ -302,7 +343,12 @@
         chosen = jnp.where(lax.div(pick, 8) + first == target, 1.0, 0.0)
         return dot_exact(dot_exact(ones, sums_ref[...], NT), chosen)[:1]
 
-    each(lambda d: to_p(band_peer(d), band_peer(d)).wait_recv())
+    def hand_on_p(d):
+        to_p(chip_peer(d), chip_peer(d)).wait_recv()
+        hand_p(chip_peer(d)).start()
+
+    chips(hand_on_p)
+    chips(lambda d: hand_p(lax.rem(sibling + 2 * d, BANDS)).wait_recv(), 0)
     overlap_row = gram_row(own, 32)
 
     each(lambda d: to_d(pencil_peer(d), pencil_peer(d)).wait_recv())
@@ -313,9 +359,9 @@
         own_h = own_h + dot3(
             (back[0][rows], back[1][rows]), (forward_ref[0, :, cols], forward_ref[1, :, cols])
         )
-    own_h_ref[...] = own_h
-    each(lambda d: to_h(band_peer(d), band).start())
     bands_h_ref[band] = own_h
+    chips(lambda d: to_h(chip_peer(d), band).start())
+    hand_h(band).start()
 
     send_g[...] = gram_row(own_h, 0) + overlap_row
     each(lambda d: to_g(pencil_peer(d), pencil).start())
@@ -324,6 +370,9 @@
     row_ref[...] = jnp.sum(recv_g[...], axis=0) / float(STICKS * GRID)
     each(lambda d: to_r(band_peer(d), band).start())
     recv_r[band] = row_ref[...]
+    for d in (1, 7, 2, 6, 3, 5, 4):
+        to_h(chip_peer(d), chip_peer(d)).wait_recv()
+        hand_h(chip_peer(d)).start()
 
     x_r, x_i = ritz_ref[0], ritz_ref[1]
     xt = jnp.concatenate([x_r.T, x_i.T], axis=1)
@@ -365,34 +414,53 @@
         return narrow(along - turned(across))[:, : 2 * GRID]
 
     refined_ref[0] = rotate(bands_ref)
-    each(lambda d: to_h(band_peer(d), band_peer(d)).wait_recv())
+    chips(lambda d: hand_h(lax.rem(sibling + 2 * d, BANDS)).wait_recv(), 0)
     refined_h_ref[0] = rotate(bands_h_ref)
 
     def finish(d):
         to_b(pencil_peer(d), pencil).wait_send()
         to_d(pencil_peer(d), pencil).wait_send()
         to_g(pencil_peer(d), pencil).wait_send()
-        to_p(band_peer(d), band).wait_send()
-        to_h(band_peer(d), band).wait_send()
         to_r(band_peer(d), band).wait_send()
 
     each(finish)
+    chips(lambda d: to_p(chip_peer(d), band).wait_send())
+    chips(lambda d: to_h(chip_peer(d), band).wait_send())
+    chips(lambda d: hand_p(chip_peer(d)).wait_send(), 0)
+    chips(lambda d: hand_h(chip_peer(d)).wait_send(), 0)
+
+
+def emit(*refs):
+    sem = refs[6]
+    copies = [pltpu.make_async_copy(refs[k], refs[3 + k], sem.at[k]) for k in range(3)]
+    for copy in copies:
+        copy.start()
+    for copy in copies:
+        copy.wait()
 
 
 def shards(coeffs, columns, potential, ritz_vectors):
     inverse, forward = z_tables()
     vmem = pl.BlockSpec(memory_space=pltpu.VMEM)
-    refined, refined_h, values = pl.pallas_call(
+    outs = (
+        jax.ShapeDtypeStruct((1, OWN, 2 * GRID), f32),
+        jax.ShapeDtypeStruct((1, OWN, 2 * GRID), f32),
+        jax.ShapeDtypeStruct((1, BANDS), f32),
+    )
+    results = pl.pallas_call(
         kernel,
-        out_shape=(
-            jax.ShapeDtypeStruct((1, OWN, 2 * GRID), f32),
-            jax.ShapeDtypeStruct((1, OWN, 2 * GRID), f32),
-            jax.ShapeDtypeStruct((1, BANDS), f32),
-        ),
-        in_specs=[vmem] * 7,
+        out_shape=outs,
+        in_specs=[pl.BlockSpec(memory_space=pltpu.HBM)] * 7,
         out_specs=(vmem,) * 3,
         scratch_shapes=[
-            pltpu.VMEM((OWN, 256), f32),
+            pltpu.VMEM((1, OWN, 2 * GRID), f32),
+            pltpu.VMEM((1, STICKS), jnp.int32),
+            pltpu.VMEM((PLANES, GRID * GRID), f32),
+            pltpu.VMEM((2, BANDS, BANDS), f32),
+            pltpu.VMEM((2, 64, 1024), bf16),
+            pltpu.VMEM((2, 64, 1024), bf16),
+            pltpu.VMEM((3, 256, 128), bf16),
+            pltpu.SemaphoreType.DMA((7,)),
             pltpu.VMEM((OWN, 256), f32),
             pltpu.VMEM((2, 128, 1024), bf16),
             pltpu.VMEM((16, 4, 128), f32),
@@ -404,9 +472,9 @@
             pltpu.VMEM((2, 256, 1024), bf16),
             pltpu.VMEM((GRID, 8, 128), f32),
             pltpu.VMEM((2, 896, 1024), bf16),
+            pltpu.VMEM((2, 896, 256), bf16),
             pltpu.VMEM((896, 1024), f32),
             pltpu.VMEM((BANDS, OWN, 256), f32),
-            pltpu.VMEM((OWN, 256), f32),
             pltpu.VMEM((BANDS, OWN, 256), f32),
             pltpu.VMEM((256, 256), f32),
             pltpu.VMEM((1, 128), f32),
@@ -414,9 +482,9 @@
             pltpu.VMEM((1, 128), f32),
             pltpu.VMEM((16, 1, 128), f32),
         ]
-        + [pltpu.SemaphoreType.DMA((16,))] * 12,
+        + [pltpu.SemaphoreType.DMA((16,))] * 14,
         compiler_params=pltpu.CompilerParams(
-            collective_id=0, has_side_effects=True, vmem_limit_bytes=48 * 2**20
+            collective_id=0, has_side_effects=True, vmem_limit_bytes=62 * 2**20
         ),
     )(
         coeffs,
@@ -427,6 +495,14 @@
         jnp.asarray(forward),
         jnp.asarray(wave_table()),
     )
+    anywhere = pl.BlockSpec(memory_space=pl.ANY)
+    refined, refined_h, values = pl.pallas_call(
+        emit,
+        out_shape=outs,
+        in_specs=[anywhere] * 3,
+        out_specs=(anywhere,) * 3,
+        scratch_shapes=[pltpu.SemaphoreType.DMA((3,))],
+    )(*results)
     return refined, refined_h, values.reshape(BANDS)
 
 

time: 53.6 us -> 43.3 us (0.81)
  local copies, waits for them, and re-layouts: 7.71 us -> 0 us
  Pallas kernels: 44.9 us -> 42.5 us
    unnamed x17 -> x0, local copies, waits for them, and re-layouts: 7.71 us -> none
    pallas_call x1 -> x2, Pallas kernels: 44.9 us -> 42.5 us  [the longest x1 39.4 us: shards(): pl.pallas_call(kernel, out_shape=outs, in_specs=[pl.BlockSpec(memory_spac...]
where the time goes in v2:
time: 43.3 us; the launch traced here: 43.2 us
  Pallas kernels  42.5 us (98%)
  between operations  0.64 us (1%)
    pallas_call x1, Pallas kernels, shards(): pl.pallas_call(kernel, out_shape=outs, in_specs=[pl.BlockSpec(memory_spac...  39.4 us
    pallas_call x1, Pallas kernels, shards(): pl.pallas_call(emit, out_shape=outs, in_specs=[anywhere] * 3, out_specs=(...  3.13 us

profile of v2, /device:TPU:1, one launch (start us, length us, event | category | flops | bytes accessed | tf_op | source)
XLA Modules:
  0.0 43.2 jit_solution(9072371348298926274)
XLA Ops:
  0.6 39.4 %shard_map.94 = (f32[1,32,224]{2,1,0:T(8,128)}, f32[1,32,224]{2,1,0:T(8,128)}, f32[1,16]{1,0:T(1,128)}) custom-call(f32[1,32,224]{2,1,0:T(8,128)} %coeffs_hbm.1, s32[1,512]{1,0:T(1,128)} %bitcast.2, f32[7,12544]{1,0:T(8,128)} %potential_hbm.1, f32[2,16,16]{2,1,0:T(8,128)} %ritz_hbm.1, bf16[2,64,1024]{2,1,0:T(8,128)(2,1)} %constant.6.clone.inverse_hbm, ...), custom_call_target="tpu_custom_call" | custom-call | tf_op jit(solution)/shard_map/pallas_call | solution.py:450
  40.0 3.1 %shard_map.95 = (f32[1,32,224]{2,1,0:T(8,128)}, f32[1,32,224]{2,1,0:T(8,128)}, f32[1,16]{1,0:T(1,128)}) custom-call(f32[1,32,224]{2,1,0:T(8,128)} %get-tuple-element.9.refs_0_, f32[1,32,224]{2,1,0:T(8,128)} %get-tuple-element.10.refs_1_, f32[1,16]{1,0:T(1,128)} %get-tuple-element.11.refs_2_), custom_call_target="tpu_custom_call" | custom-call | tf_op jit(solution)/shard_map/pallas_call | solution.py:499

commit v3 on v2

--- a/solution.py
+++ b/solution.py
@@ -431,12 +431,8 @@
 
 
 def emit(*refs):
-    sem = refs[6]
-    copies = [pltpu.make_async_copy(refs[k], refs[3 + k], sem.at[k]) for k in range(3)]
-    for copy in copies:
-        copy.start()
-    for copy in copies:
-        copy.wait()
+    for k in range(3):
+        refs[3 + k][...] = refs[k][...]
 
 
 def shards(coeffs, columns, potential, ritz_vectors):
@@ -449,7 +445,7 @@
     )
     results = pl.pallas_call(
         kernel,
-        out_shape=outs,
+        out_shape=tuple(pltpu.VMEM(o.shape, f32) for o in outs),
         in_specs=[pl.BlockSpec(memory_space=pltpu.HBM)] * 7,
         out_specs=(vmem,) * 3,
         scratch_shapes=[
@@ -499,9 +495,9 @@
     refined, refined_h, values = pl.pallas_call(
         emit,
         out_shape=outs,
-        in_specs=[anywhere] * 3,
-        out_specs=(anywhere,) * 3,
-        scratch_shapes=[pltpu.SemaphoreType.DMA((3,))],
+        in_specs=[vmem] * 3,
+        out_specs=(vmem,) * 3,
+        compiler_params=pltpu.CompilerParams(vmem_limit_bytes=2**20),
     )(*results)
     return refined, refined_h, values.reshape(BANDS)
 

time: 43.3 us -> 40.2 us (0.928)
  Pallas kernels: 42.5 us -> 39.4 us
    pallas_call x2, Pallas kernels: 42.5 us -> 39.4 us  [the longest x1 38.8 us: shards(): pl.pallas_call(kernel, out_shape=tuple((pltpu.VMEM(o.shape, f32) for o in...]
where the time goes in v3:
time: 40.2 us; the launch traced here: 40.1 us
  Pallas kernels  39.4 us (98%)
  between operations  0.64 us (2%)
    pallas_call x1, Pallas kernels, shards(): pl.pallas_call(kernel, out_shape=tuple((pltpu.VMEM(o.shape, f32) for o in...  38.8 us

profile of v3, /device:TPU:1, one launch (start us, length us, event | category | flops | bytes accessed | tf_op | source)
XLA Modules:
  0.0 40.1 jit_solution(260262597667037225)
XLA Ops:
  0.6 38.8 %shard_map.94 = (f32[1,32,224]{2,1,0:T(8,128)S(1)}, f32[1,32,224]{2,1,0:T(8,128)S(1)}, f32[1,16]{1,0:T(1,128)S(1)}) custom-call(f32[1,32,224]{2,1,0:T(8,128)} %coeffs_hbm.1, s32[1,512]{1,0:T(1,128)} %bitcast.2, f32[7,12544]{1,0:T(8,128)} %potential_hbm.1, f32[2,16,16]{2,1,0:T(8,128)} %ritz_hbm.1, bf16[2,64,1024]{2,1,0:T(8,128)(2,1)} %constant.6.clone.inverse_hbm, ...), custom_call_target="tpu_custom_call" | custom-call | tf_op jit(solution)/shard_map/pallas_call | solution.py:446
  39.4 0.6 %shard_map.95 = (f32[1,32,224]{2,1,0:T(8,128)}, f32[1,32,224]{2,1,0:T(8,128)}, f32[1,16]{1,0:T(1,128)}) custom-call(f32[1,32,224]{2,1,0:T(8,128)S(1)} %get-tuple-element.9.refs_0_, f32[1,32,224]{2,1,0:T(8,128)S(1)} %get-tuple-element.10.refs_1_, f32[1,16]{1,0:T(1,128)S(1)} %get-tuple-element.11.refs_2_), custom_call_target="tpu_custom_call" | custom-call | tf_op jit(solution)/shard_map/pallas_call | solution.py:495

commit v4 on v3

--- a/solution.py
+++ b/solution.py
@@ -16,6 +16,7 @@
 STICKS = 512
 OWN = 32
 RADIUS = 28
+NEAR = (1, 7, 2, 6, 3, 5, 4)
 
 f32 = jnp.float32
 bf16 = jnp.bfloat16
@@ -43,8 +44,7 @@
 
 
 def z_tables():
-    inverse = np.zeros((64, 4, 256))
-    forward = np.zeros((64, 4, 256))
+    table = np.zeros((4, PENCILS, 4, 256))
     k = np.arange(GRID)
     for p in range(PENCILS):
         for r in range(4):
@@ -55,12 +55,10 @@
                 angle = 2.0 * np.pi * ((k * (PLANES * p + z)) % GRID) / GRID
                 cosine, sine = np.cos(angle), np.sin(angle)
                 real = q // 2 == 0
-                row = 4 * p + r
-                inverse[row, q, :GRID] = cosine if real else sine
-                inverse[row, q, 128 : 128 + GRID] = -sine if real else cosine
-                forward[row, q, :GRID] = cosine if real else sine
-                forward[row, q, 128 : 128 + GRID] = -sine if real else cosine
-    return parts_of(inverse.reshape(64, 1024), 2), parts_of(forward.reshape(64, 1024) / float(GRID) ** 3, 2)
+                table[q, p, r, :GRID] = cosine if real else sine
+                table[q, p, r, 128 : 128 + GRID] = -sine if real else cosine
+    table = table.reshape(256, 256)
+    return parts_of(table, 2), parts_of(table / float(GRID) ** 3, 2)
 
 
 def split(x):
@@ -108,7 +106,7 @@
     coeffs_hbm, columns_hbm, potential_hbm, ritz_hbm, inverse_hbm, forward_hbm, wave_hbm,
     refined_ref, refined_h_ref, values_ref,
     coeffs_ref, columns_ref, potential_ref, ritz_ref, inverse_ref, forward_ref, wave_ref, sem_in,
-    pad_ref, block_ref, send_b, recv_b, send_d, recv_d, psi_ref, a_ref, t_ref, v_ref, p_ref, w_ref, c_ref,
+    pad_ref, rows_ref, scale_ref, send_b, recv_b, send_d, recv_d, psi_ref, a_ref, t_ref, v_ref, p_ref, w_ref, c_ref,
     bands_ref, bands_h_ref, sums_ref, send_g, recv_g, row_ref, recv_r,
     sem_sb, sem_rb, sem_sd, sem_rd, sem_sp, sem_fp, sem_rp, sem_sh, sem_fh, sem_rh, sem_sg, sem_rg, sem_sr, sem_rr,
 ):
@@ -122,11 +120,8 @@
         return lax.rem(band + d, BANDS)
 
     def each(body):
-        def step(d, carry):
+        for d in range(1, 16):
             body(d)
-            return carry
-
-        lax.fori_loop(1, 16, step, 0)
 
     def to_b(p, mine):
         return pltpu.make_async_remote_copy(
@@ -200,19 +195,20 @@
     each(greet)
     for load in loads[2:]:
         load.start()
+    pad_ref[...] = jnp.zeros_like(pad_ref)
+    rows_ref[...] = jnp.zeros_like(rows_ref)
     for load in loads[:2]:
         load.wait()
 
-    pad_ref[...] = jnp.zeros_like(pad_ref)
     pad_ref[:, : 2 * GRID] = coeffs_ref[0]
     own = wide(pad_ref[...])
     bands_ref[band] = own
-    own_high, own_low = split(own)
-    block_ref[...] = jnp.zeros_like(block_ref)
-    for q in range(4):
-        block_ref[0, 32 * q : 32 * q + 32, 256 * q : 256 * q + 256] = own_high
-        block_ref[1, 32 * q : 32 * q + 32, 256 * q : 256 * q + 256] = own_low
-    packed = dot3((inverse_ref[0], inverse_ref[1]), (block_ref[0], block_ref[1]), NT)
+    group = lax.div(lax.broadcasted_iota(jnp.int32, (64, 128), 1), 32)
+    copies = jnp.concatenate([own] * 4, axis=0)
+    planes = dot3((inverse_ref[0], inverse_ref[1]), split(copies), NT)
+    packed = planes[:64]
+    for q in range(1, 4):
+        packed = jnp.where(group == q, planes[64 * q : 64 * q + 64], packed)
     send_b[...] = packed.reshape(PENCILS, 4, 128)
 
     pl.semaphore_wait(barrier, 30)
@@ -256,7 +252,7 @@
 
     each(lambda d: to_b(pencil_peer(d), pencil_peer(d)).wait_recv())
     got = recv_b[...].reshape(4, 16, 128)
-    group = lax.div(lax.broadcasted_iota(jnp.int32, (16, 128), 1), 32)
+    group = group[:16]
     for q in range(4):
         out = got[0] if q == 0 else pltpu.roll(got[0], (-32 * q) % 128, 1)
         for p in range(1, 4):
@@ -323,25 +319,22 @@
     each(lambda d: to_d(pencil_peer(d), pencil).start())
     recv_d[pencil] = send_d[slot_of(pencil)]
 
-    pick = lax.broadcasted_iota(jnp.int32, (256, 128), 0)
-    ones = jnp.ones((8, 256), f32)
-
-    def gram_row(values, first):
+    def gram_rows(values, first):
         other = turned(values)
 
-        def one(i, carry):
-            member = bands_ref[i]
-            real, imag = member * values, member * other
-            rows = pl.ds(pl.multiple_of(8 * i, 8), 8)
-            later = pl.ds(pl.multiple_of(128 + 8 * i, 8), 8)
-            sums_ref[rows, :] = (real[:8] + real[8:16]) + (real[16:24] + real[24:])
-            sums_ref[later, :] = (imag[:8] + imag[8:16]) + (imag[16:24] + imag[24:])
+        def one(n, carry):
+            for k in range(4):
+                i = 4 * n + k
+                member = bands_ref[i]
+                for part, factor in enumerate((values, other)):
+                    products = member * factor
+                    folded = (products[:8] + products[8:16]) + (products[16:24] + products[24:])
+                    rows = pl.ds(pl.multiple_of(128 * part + 8 * i, 8), 8)
+                    sums_ref[rows, :] = folded[:, :128] + folded[:, 128:]
             return carry
 
-        lax.fori_loop(0, BANDS, one, 0)
-        target = lax.broadcasted_iota(jnp.int32, (256, 128), 1)
-        chosen = jnp.where(lax.div(pick, 8) + first == target, 1.0, 0.0)
-        return dot_exact(dot_exact(ones, sums_ref[...], NT), chosen)[:1]
+        lax.fori_loop(0, 4, one, 0)
+        rows_ref[first : first + 32, :] = jnp.sum(sums_ref[...].reshape(32, 8, 128), axis=1)
 
     def hand_on_p(d):
         to_p(chip_peer(d), chip_peer(d)).wait_recv()
@@ -349,28 +342,30 @@
 
     chips(hand_on_p)
     chips(lambda d: hand_p(lax.rem(sibling + 2 * d, BANDS)).wait_recv(), 0)
-    overlap_row = gram_row(own, 32)
+    gram_rows(own, 32)
 
     each(lambda d: to_d(pencil_peer(d), pencil_peer(d)).wait_recv())
-    back = split(recv_d[...].reshape(64, 128).T)
-    own_h = kinetic * own
-    for q in range(4):
-        rows, cols = slice(32 * q, 32 * q + 32), slice(256 * q, 256 * q + 256)
-        own_h = own_h + dot3(
-            (back[0][rows], back[1][rows]), (forward_ref[0, :, cols], forward_ref[1, :, cols])
-        )
+    arrived = recv_d[...].reshape(64, 128)
+    back = jnp.concatenate([arrived, arrived], axis=0).T
+    low_half = lax.broadcasted_iota(jnp.int32, (OWN, 128), 1) < 64
+    lined = jnp.concatenate(
+        [jnp.where(low_half, back[64 * h : 64 * h + 32], back[64 * h + 32 : 64 * h + 64]) for h in range(2)], axis=1
+    )
+    own_h = kinetic * own + dot3(split(lined), (forward_ref[0], forward_ref[1]))
     bands_h_ref[band] = own_h
-    chips(lambda d: to_h(chip_peer(d), band).start())
+    for d in NEAR[::-1]:
+        to_h(chip_peer(d), band).start()
     hand_h(band).start()
 
-    send_g[...] = gram_row(own_h, 0) + overlap_row
+    gram_rows(own_h, 0)
+    send_g[...] = dot_exact(jnp.ones((8, 128), f32), rows_ref[...], NT)[:1]
     each(lambda d: to_g(pencil_peer(d), pencil).start())
     recv_g[pencil] = send_g[...]
     each(lambda d: to_g(pencil_peer(d), pencil_peer(d)).wait_recv())
     row_ref[...] = jnp.sum(recv_g[...], axis=0) / float(STICKS * GRID)
     each(lambda d: to_r(band_peer(d), band).start())
     recv_r[band] = row_ref[...]
-    for d in (1, 7, 2, 6, 3, 5, 4):
+    for d in NEAR:
         to_h(chip_peer(d), chip_peer(d)).wait_recv()
         hand_h(chip_peer(d)).start()
 
@@ -404,18 +399,29 @@
     new_r = jnp.sum(x_r * u_r - x_i * u_i, axis=1, keepdims=True)
     new_i = jnp.sum(x_r * u_i + x_i * u_r, axis=1, keepdims=True)
 
-    def rotate(members):
-        along = jnp.zeros((OWN, 256), f32)
-        across = jnp.zeros((OWN, 256), f32)
-        for i in range(BANDS):
-            member = members[i]
-            along = along + new_r[i : i + 1] * member
-            across = across + new_i[i : i + 1] * member
-        return narrow(along - turned(across))[:, : 2 * GRID]
-
-    refined_ref[0] = rotate(bands_ref)
-    chips(lambda d: hand_h(lax.rem(sibling + 2 * d, BANDS)).wait_recv(), 0)
-    refined_h_ref[0] = rotate(bands_h_ref)
+    scale_ref[0] = jnp.broadcast_to(new_r, (BANDS, 256))
+    scale_ref[1] = jnp.broadcast_to(new_i, (BANDS, 256))
+
+    def add(sums, i, members):
+        member = members[i]
+        return sums[0] + scale_ref[0, pl.ds(i, 1), :] * member, sums[1] + scale_ref[1, pl.ds(i, 1), :] * member
+
+    def rotated(sums):
+        return narrow(sums[0] - turned(sums[1]))[:, : 2 * GRID]
+
+    empty = (jnp.zeros((OWN, 256), f32),) * 2
+    sums = empty
+    for i in range(BANDS):
+        sums = add(sums, i, bands_ref)
+    refined_ref[0] = rotated(sums)
+    sums = empty
+    for d in range(8):
+        sums = add(sums, chip_peer(d), bands_h_ref)
+    for d in (0,) + NEAR:
+        i = lax.rem(sibling + 2 * d, BANDS)
+        hand_h(i).wait_recv()
+        sums = add(sums, i, bands_h_ref)
+    refined_h_ref[0] = rotated(sums)
 
     def finish(d):
         to_b(pencil_peer(d), pencil).wait_send()
@@ -453,12 +459,13 @@
             pltpu.VMEM((1, STICKS), jnp.int32),
             pltpu.VMEM((PLANES, GRID * GRID), f32),
             pltpu.VMEM((2, BANDS, BANDS), f32),
-            pltpu.VMEM((2, 64, 1024), bf16),
-            pltpu.VMEM((2, 64, 1024), bf16),
+            pltpu.VMEM((2, 256, 256), bf16),
+            pltpu.VMEM((2, 256, 256), bf16),
             pltpu.VMEM((3, 256, 128), bf16),
             pltpu.SemaphoreType.DMA((7,)),
             pltpu.VMEM((OWN, 256), f32),
-            pltpu.VMEM((2, 128, 1024), bf16),
+            pltpu.VMEM((128, 128), f32),
+            pltpu.VMEM((2, BANDS, 256), f32),
             pltpu.VMEM((16, 4, 128), f32),
             pltpu.VMEM((16, 4, 128), f32),
             pltpu.VMEM((16, 4, 128), f32),
@@ -472,7 +479,7 @@
             pltpu.VMEM((896, 1024), f32),
             pltpu.VMEM((BANDS, OWN, 256), f32),
             pltpu.VMEM((BANDS, OWN, 256), f32),
-            pltpu.VMEM((256, 256), f32),
+            pltpu.VMEM((256, 128), f32),
             pltpu.VMEM((1, 128), f32),
             pltpu.VMEM((16, 1, 128), f32),
             pltpu.VMEM((1, 128), f32),

time: 40.2 us -> 39.6 us (0.985)
  Pallas kernels: 39.4 us -> 38.8 us
    pallas_call x1, Pallas kernels: 38.8 us -> 38.2 us  [shards(): pl.pallas_call(kernel, out_shape=tuple((pltpu.VMEM(o.shape, f32) for o in...]
where the time goes in v4:
time: 39.6 us; the launch traced here: 39.5 us
  Pallas kernels  38.8 us (98%)
  between operations  0.64 us (2%)
    pallas_call x1, Pallas kernels, shards(): pl.pallas_call(kernel, out_shape=tuple((pltpu.VMEM(o.shape, f32) for o in...  38.2 us

profile of v4, /device:TPU:1, one launch (start us, length us, event | category | flops | bytes accessed | tf_op | source)
XLA Modules:
  0.0 39.5 jit_solution(1504179949552219508)
XLA Ops:
  0.6 38.2 %shard_map.94 = (f32[1,32,224]{2,1,0:T(8,128)S(1)}, f32[1,32,224]{2,1,0:T(8,128)S(1)}, f32[1,16]{1,0:T(1,128)S(1)}) custom-call(f32[1,32,224]{2,1,0:T(8,128)} %coeffs_hbm.1, s32[1,512]{1,0:T(1,128)} %bitcast.2, f32[7,12544]{1,0:T(8,128)} %potential_hbm.1, f32[2,16,16]{2,1,0:T(8,128)} %ritz_hbm.1, bf16[2,256,256]{2,1,0:T(8,128)(2,1)} %constant.6.clone.inverse_hbm, ...), custom_call_target="tpu_custom_call" | custom-call | tf_op jit(solution)/shard_map/pallas_call | solution.py:452
  38.8 0.6 %shard_map.95 = (f32[1,32,224]{2,1,0:T(8,128)}, f32[1,32,224]{2,1,0:T(8,128)}, f32[1,16]{1,0:T(1,128)}) custom-call(f32[1,32,224]{2,1,0:T(8,128)S(1)} %get-tuple-element.9.refs_0_, f32[1,32,224]{2,1,0:T(8,128)S(1)} %get-tuple-element.10.refs_1_, f32[1,16]{1,0:T(1,128)S(1)} %get-tuple-element.11.refs_2_), custom_call_target="tpu_custom_call" | custom-call | tf_op jit(solution)/shard_map/pallas_call | solution.py:502

commit v5 on v4

--- a/solution.py
+++ b/solution.py
@@ -17,6 +17,16 @@
 OWN = 32
 RADIUS = 28
 NEAR = (1, 7, 2, 6, 3, 5, 4)
+
+
+def hops(step, size):
+    return min(step, size - step)
+
+
+PENCIL_STEPS = sorted(
+    [(dx, dy) for dx in range(4) for dy in range(4) if dx or dy], key=lambda d: -hops(d[0], 4) - hops(d[1], 4)
+)
+BAND_STEPS = sorted([(dz, other) for dz in range(8) for other in range(2) if dz or other], key=lambda d: -hops(d[0], 8))
 
 f32 = jnp.float32
 bf16 = jnp.bfloat16
@@ -113,11 +123,16 @@
     pencil = lax.axis_index("pencil")
     band = lax.axis_index("band")
 
+    x_own, y_own = lax.div(pencil, 4), lax.rem(pencil, 4)
+
     def pencil_peer(d):
-        return lax.rem(pencil + d, PENCILS)
+        dx, dy = PENCIL_STEPS[d - 1]
+        return 4 * lax.rem(x_own + dx, 4) + lax.rem(y_own + dy, 4)
 
     def band_peer(d):
-        return lax.rem(band + d, BANDS)
+        dz, other = BAND_STEPS[d - 1]
+        core = lax.rem(band, 2)
+        return lax.rem(2 * (lax.div(band, 2) + dz), BANDS) + (1 - core if other else core)
 
     def each(body):
         for d in range(1, 16):
@@ -267,17 +282,18 @@
         return a_ref[pl.ds(x, 1), :], a_ref[pl.ds(128 + x, 1), :]
 
     def spread(n, carry):
-        real, imag = [], []
-        for k in range(2):
-            a_r, a_i = phases(2 * n + k)
-            real.append(a_r * psi_r - a_i * psi_i)
-            imag.append(a_r * psi_i + a_i * psi_r)
-        rows = pl.ds(pl.multiple_of(16 * n, 16), 16)
-        p_ref[0, rows, :STICKS], p_ref[1, rows, :STICKS] = split(jnp.concatenate(real, axis=0))
-        p_ref[0, rows, STICKS:], p_ref[1, rows, STICKS:] = split(jnp.concatenate(imag, axis=0))
+        for pair in range(4):
+            real, imag = [], []
+            for k in range(2):
+                a_r, a_i = phases(8 * n + 2 * pair + k)
+                real.append(a_r * psi_r - a_i * psi_i)
+                imag.append(a_r * psi_i + a_i * psi_r)
+            rows = pl.ds(pl.multiple_of(64 * n + 16 * pair, 16), 16)
+            p_ref[0, rows, :STICKS], p_ref[1, rows, :STICKS] = split(jnp.concatenate(real, axis=0))
+            p_ref[0, rows, STICKS:], p_ref[1, rows, STICKS:] = split(jnp.concatenate(imag, axis=0))
         return carry
 
-    lax.fori_loop(0, 56, spread, 0)
+    lax.fori_loop(0, 14, spread, 0)
 
     u = dot3((p_ref[0], p_ref[1]), (t_ref[0], t_ref[1]), NT)
     v = v_ref[...].reshape(896, 128)
@@ -294,8 +310,8 @@
 
     def collect(n, carry):
         w_r, w_i = carry
-        for k in range(4):
-            x = 4 * n + k
+        for k in range(8):
+            x = 8 * n + k
             a_r, a_i = phases(x)
             rows = pl.ds(pl.multiple_of(8 * x, 8), 8)
             c_r, c_i = c_ref[rows, :STICKS], c_ref[rows, STICKS:]
@@ -304,7 +320,7 @@
         return w_r, w_i
 
     zero = jnp.zeros((8, STICKS), f32)
-    sums = lax.fori_loop(0, 28, collect, (zero, zero))
+    sums = lax.fori_loop(0, 14, collect, (zero, zero))
 
     outs = []
     for q in range(4):

time: 39.6 us -> 39.1 us (0.987)
  Pallas kernels: 38.8 us -> 38.3 us
    pallas_call x1, Pallas kernels: 38.2 us -> 37.7 us  [shards(): pl.pallas_call(kernel, out_shape=tuple((pltpu.VMEM(o.shape, f32) for o in...]
where the time goes in v5:
time: 39.1 us; the launch traced here: 39 us
  Pallas kernels  38.3 us (98%)
  between operations  0.64 us (2%)
    pallas_call x1, Pallas kernels, shards(): pl.pallas_call(kernel, out_shape=tuple((pltpu.VMEM(o.shape, f32) for o in...  37.7 us

profile of v5, /device:TPU:1, one launch (start us, length us, event | category | flops | bytes accessed | tf_op | source)
XLA Modules:
  0.0 39.0 jit_solution(11262888243516256191)
XLA Ops:
  0.6 37.7 %shard_map.94 = (f32[1,32,224]{2,1,0:T(8,128)S(1)}, f32[1,32,224]{2,1,0:T(8,128)S(1)}, f32[1,16]{1,0:T(1,128)S(1)}) custom-call(f32[1,32,224]{2,1,0:T(8,128)} %coeffs_hbm.1, s32[1,512]{1,0:T(1,128)} %bitcast.2, f32[7,12544]{1,0:T(8,128)} %potential_hbm.1, f32[2,16,16]{2,1,0:T(8,128)} %ritz_hbm.1, bf16[2,256,256]{2,1,0:T(8,128)(2,1)} %constant.6.clone.inverse_hbm, ...), custom_call_target="tpu_custom_call" | custom-call | tf_op jit(solution)/shard_map/pallas_call | solution.py:468
  38.3 0.6 %shard_map.95 = (f32[1,32,224]{2,1,0:T(8,128)}, f32[1,32,224]{2,1,0:T(8,128)}, f32[1,16]{1,0:T(1,128)}) custom-call(f32[1,32,224]{2,1,0:T(8,128)S(1)} %get-tuple-element.9.refs_0_, f32[1,32,224]{2,1,0:T(8,128)S(1)} %get-tuple-element.10.refs_1_, f32[1,16]{1,0:T(1,128)S(1)} %get-tuple-element.11.refs_2_), custom_call_target="tpu_custom_call" | custom-call | tf_op jit(solution)/shard_map/pallas_call | solution.py:518

commit v6 on v5

--- a/solution.py
+++ b/solution.py
@@ -360,6 +360,9 @@
     chips(lambda d: hand_p(lax.rem(sibling + 2 * d, BANDS)).wait_recv(), 0)
     gram_rows(own, 32)
 
+    each(lambda d: to_b(pencil_peer(d), pencil).wait_send())
+    chips(lambda d: to_p(chip_peer(d), band).wait_send())
+    chips(lambda d: hand_p(chip_peer(d)).wait_send(), 0)
     each(lambda d: to_d(pencil_peer(d), pencil_peer(d)).wait_recv())
     arrived = recv_d[...].reshape(64, 128)
     back = jnp.concatenate([arrived, arrived], axis=0).T
@@ -377,6 +380,7 @@
     send_g[...] = dot_exact(jnp.ones((8, 128), f32), rows_ref[...], NT)[:1]
     each(lambda d: to_g(pencil_peer(d), pencil).start())
     recv_g[pencil] = send_g[...]
+    each(lambda d: to_d(pencil_peer(d), pencil).wait_send())
     each(lambda d: to_g(pencil_peer(d), pencil_peer(d)).wait_recv())
     row_ref[...] = jnp.sum(recv_g[...], axis=0) / float(STICKS * GRID)
     each(lambda d: to_r(band_peer(d), band).start())
@@ -390,13 +394,16 @@
     conj = jnp.concatenate(
         [jnp.concatenate([x_r, -x_i], axis=1), jnp.concatenate([x_i, x_r], axis=1)], axis=0
     )
+    each(lambda d: to_g(pencil_peer(d), pencil).wait_send())
+    chips(lambda d: to_h(chip_peer(d), band).wait_send())
+    each(lambda d: to_r(band_peer(d), band).wait_send())
     each(lambda d: to_r(band_peer(d), band_peer(d)).wait_recv())
     grams = recv_r[...].reshape(BANDS, 128)
     lane = lax.broadcasted_iota(jnp.int32, (BANDS, 128), 1)
     swapped = jnp.where(lax.rem(lane, 32) < 16, -pltpu.roll(grams, 112, 1), pltpu.roll(grams, 16, 1))
     half = dot_exact(xt, jnp.concatenate([grams, swapped], axis=0))
-    energy = dot_exact(half[:, :32], conj)
-    metric = dot_exact(half[:, 32:64], conj)
+    pair = dot_exact(jnp.concatenate([half[:, :32], half[:, 32:64]], axis=0), conj)
+    energy, metric = pair[:BANDS], pair[BANDS:]
     row16 = lax.broadcasted_iota(jnp.int32, (BANDS, 16), 0)
     diagonal = row16 == lax.broadcasted_iota(jnp.int32, (BANDS, 16), 1)
     ratio = jnp.where(diagonal, energy[:, :16] / metric[:, :16], 0.0)
@@ -439,16 +446,6 @@
         sums = add(sums, i, bands_h_ref)
     refined_h_ref[0] = rotated(sums)
 
-    def finish(d):
-        to_b(pencil_peer(d), pencil).wait_send()
-        to_d(pencil_peer(d), pencil).wait_send()
-        to_g(pencil_peer(d), pencil).wait_send()
-        to_r(band_peer(d), band).wait_send()
-
-    each(finish)
-    chips(lambda d: to_p(chip_peer(d), band).wait_send())
-    chips(lambda d: to_h(chip_peer(d), band).wait_send())
-    chips(lambda d: hand_p(chip_peer(d)).wait_send(), 0)
     chips(lambda d: hand_h(chip_peer(d)).wait_send(), 0)
 
 

time: 39.1 us -> 38.6 us (0.987)
  Pallas kernels: 38.3 us -> 37.9 us
    pallas_call x1, Pallas kernels: 37.7 us -> 37.2 us  [shards(): pl.pallas_call(kernel, out_shape=tuple((pltpu.VMEM(o.shape, f32) for o in...]
where the time goes in v6:
time: 38.6 us; the launch traced here: 38.5 us
  Pallas kernels  37.9 us (98%)
  between operations  0.64 us (2%)
    pallas_call x1, Pallas kernels, shards(): pl.pallas_call(kernel, out_shape=tuple((pltpu.VMEM(o.shape, f32) for o in...  37.2 us

profile of v6, /device:TPU:1, one launch (start us, length us, event | category | flops | bytes accessed | tf_op | source)
XLA Modules:
  0.0 38.5 jit_solution(5920822987651248628)
XLA Ops:
  0.6 37.2 %shard_map.94 = (f32[1,32,224]{2,1,0:T(8,128)S(1)}, f32[1,32,224]{2,1,0:T(8,128)S(1)}, f32[1,16]{1,0:T(1,128)S(1)}) custom-call(f32[1,32,224]{2,1,0:T(8,128)} %coeffs_hbm.1, s32[1,512]{1,0:T(1,128)} %bitcast.2, f32[7,12544]{1,0:T(8,128)} %potential_hbm.1, f32[2,16,16]{2,1,0:T(8,128)} %ritz_hbm.1, bf16[2,256,256]{2,1,0:T(8,128)(2,1)} %constant.6.clone.inverse_hbm, ...), custom_call_target="tpu_custom_call" | custom-call | tf_op jit(solution)/shard_map/pallas_call | solution.py:465
  37.9 0.6 %shard_map.95 = (f32[1,32,224]{2,1,0:T(8,128)}, f32[1,32,224]{2,1,0:T(8,128)}, f32[1,16]{1,0:T(1,128)}) custom-call(f32[1,32,224]{2,1,0:T(8,128)S(1)} %get-tuple-element.9.refs_0_, f32[1,32,224]{2,1,0:T(8,128)S(1)} %get-tuple-element.10.refs_1_, f32[1,16]{1,0:T(1,128)S(1)} %get-tuple-element.11.refs_2_), custom_call_target="tpu_custom_call" | custom-call | tf_op jit(solution)/shard_map/pallas_call | solution.py:515

commit v7 on v6

--- a/solution.py
+++ b/solution.py
@@ -228,8 +228,6 @@
 
     pl.semaphore_wait(barrier, 30)
     each(lambda d: to_b(pencil_peer(d), pencil).start())
-    chips(lambda d: to_p(chip_peer(d), band).start())
-    hand_p(band).start()
     recv_b[slot_of(pencil)] = send_b[pencil]
     for load in loads[2:]:
         load.wait()
@@ -256,6 +254,8 @@
 
     lax.fori_loop(0, 14, lay_out, 0)
 
+    chips(lambda d: to_p(chip_peer(d), band).start())
+    hand_p(band).start()
     freq_x, freq_y = frequency(index_x), frequency(index_y)
     lateral = freq_x * freq_x + freq_y * freq_y
     stick = lax.broadcasted_iota(jnp.int32, (OWN, STICKS), 1)

time: 38.6 us -> 38.6 us (level)
  no operation moved by 1% of the time
where the time goes in v7:
time: 38.6 us; the launch traced here: 38.5 us
  Pallas kernels  37.9 us (98%)
  between operations  0.64 us (2%)
    pallas_call x1, Pallas kernels, shards(): pl.pallas_call(kernel, out_shape=tuple((pltpu.VMEM(o.shape, f32) for o in...  37.2 us

profile of v7, /device:TPU:1, one launch (start us, length us, event | category | flops | bytes accessed | tf_op | source)
XLA Modules:
  0.0 38.5 jit_solution(1100873867877229221)
XLA Ops:
  0.6 37.2 %shard_map.94 = (f32[1,32,224]{2,1,0:T(8,128)S(1)}, f32[1,32,224]{2,1,0:T(8,128)S(1)}, f32[1,16]{1,0:T(1,128)S(1)}) custom-call(f32[1,32,224]{2,1,0:T(8,128)} %coeffs_hbm.1, s32[1,512]{1,0:T(1,128)} %bitcast.2, f32[7,12544]{1,0:T(8,128)} %potential_hbm.1, f32[2,16,16]{2,1,0:T(8,128)} %ritz_hbm.1, bf16[2,256,256]{2,1,0:T(8,128)(2,1)} %constant.6.clone.inverse_hbm, ...), custom_call_target="tpu_custom_call" | custom-call | tf_op jit(solution)/shard_map/pallas_call | solution.py:465
  37.9 0.6 %shard_map.95 = (f32[1,32,224]{2,1,0:T(8,128)}, f32[1,32,224]{2,1,0:T(8,128)}, f32[1,16]{1,0:T(1,128)}) custom-call(f32[1,32,224]{2,1,0:T(8,128)S(1)} %get-tuple-element.9.refs_0_, f32[1,32,224]{2,1,0:T(8,128)S(1)} %get-tuple-element.10.refs_1_, f32[1,16]{1,0:T(1,128)S(1)} %get-tuple-element.11.refs_2_), custom_call_target="tpu_custom_call" | custom-call | tf_op jit(solution)/shard_map/pallas_call | solution.py:515
